TPU v7x, 32 devices: a whole 2x2x4 slice. The times are simulated.
32 devices in a mesh: dp: 8 (over z, y), seq: 4 (over x, core).
Axes of the slice: x: 2, y: 2, z: 4, core: 2. Of those that a mesh axis runs over, the one named last changes fastest.
Arguments:
- hidden_in: bfloat16 [512, 64, 768], P('seq', 'dp'), may hold values from -6 to 6
- lengths: int32 [64], P('dp'), may hold values from 64 to 512, as said below
- labels: int32 [64], P(('dp', 'seq')), may hold values from 0 to 2
- out_cotangent: bfloat16 [512, 64, 768], P('seq', 'dp'), may hold values from -6 to 6
- qkv_weight: bfloat16 [768, 2304], replicated, may hold values from -0.21875 to 0.21875
- out_weight: bfloat16 [768, 768], replicated, may hold values from -1.25 to 1.25
- up_weight: bfloat16 [768, 3072], replicated, may hold values from -0.21875 to 0.21875
- down_weight: bfloat16 [3072, 768], replicated, may hold values from -0.109375 to 0.109375
- pool_weight: bfloat16 [768, 768], replicated, may hold values from -0.21875 to 0.21875
- class_weight: bfloat16 [768, 3], replicated, may hold values from -1.75 to 1.75
- norm_gains: float32 [2, 768], replicated, may hold values from 0.4 to 1.6
- biases: float32 [7, 768], replicated, may hold values from -2 to 2
- up_bias: float32 [3072], replicated, may hold values from -2 to 2
- class_bias: float32 [3], replicated, may hold values from -4 to 4
Outputs:
- hidden_out: bfloat16 [512, 64, 768], P('seq', 'dp')
- ramp_logits: float32 [64, 3], P(('dp', 'seq'))
- grad_in: float32 [512, 64, 768], P('seq', 'dp')
- grad_qkv_weight: float32 [768, 2304], P(('dp', 'seq'))
- grad_out_weight: float32 [768, 768], P(('dp', 'seq'))
- grad_up_weight: float32 [768, 3072], P(('dp', 'seq'))
- grad_down_weight: float32 [3072, 768], P(('dp', 'seq'))
- grad_pool_weight: float32 [768, 768], P(('dp', 'seq'))
- grad_class_weight: float32 [768, 3], P(('dp', 'seq'))
- grad_norm_gains: float32 [2, 768], P(None, ('dp', 'seq'))
- grad_biases: float32 [7, 768], P(None, ('dp', 'seq'))
- grad_up_bias: float32 [3072], P(('dp', 'seq'))
- grad_class_bias: float32 [3], replicated
Inputs may be any that keep to these rules, and one draw needn't show every extreme that they name: `lengths`: each is at least 64; among the sequences of each index of dp, one is exactly 512 long.
All inputs are finite; a program needn't handle non-finite values.
Results may differ from a plain program's by a relative error of at most 0.012.
Values may be sent and summed in bfloat16 or wider, within the bound.
No kernel may reach another device: no remote copies, remote signals or barrier semaphores. Data moves between devices by JAX's collectives and lax.ppermute only.
A program may use at most 192 MiB of HBM per device.

v0:
```python
import jax
import jax.numpy as jnp
from jax import lax
from jax.sharding import PartitionSpec as P

HEAD_DIM = 64


eps = 1e-12
neg_big = -1e30
highest = lax.Precision.HIGHEST


def inner_dot(left_in, right_in):
    return lax.dot_general(
        left_in, right_in, (((0,), (0,)), ((), ())), preferred_element_type=jnp.float32
    )


def trans_dot(left_in, right_in):
    return lax.dot_general(
        left_in, right_in, (((1,), (1,)), ((), ())), preferred_element_type=jnp.float32
    )


def smooth_act(values):
    return jax.nn.gelu(values, approximate=False)


def norm_rows(resid, gain, shift):
    row_mean = jnp.mean(resid, axis=-1, keepdims=True)
    centred = resid - row_mean
    row_scale = lax.rsqrt(jnp.mean(centred * centred, axis=-1, keepdims=True) + eps)
    normed = centred * row_scale
    return (normed * gain + shift, normed, row_scale)


def norm_back(grad_upper, normed, row_scale, gain):
    scaled = grad_upper * gain
    mean_part = jnp.mean(scaled, axis=-1, keepdims=True)
    proj_part = jnp.mean(scaled * normed, axis=-1, keepdims=True)
    grad_lower = row_scale * (scaled - mean_part - normed * proj_part)
    return (grad_lower, jnp.sum(grad_upper * normed, axis=0), jnp.sum(grad_upper, axis=0))


def scores_of(queries, keys_in, live_keys):
    raw_scores = jnp.einsum(
        "qhd,khd->hqk", queries, keys_in, preferred_element_type=jnp.float32
    ) * HEAD_DIM ** (-0.5)
    return jnp.where(live_keys[None, None, :], raw_scores, neg_big)


def attend_one(packed):
    block_qkv, live_keys = packed
    scores = scores_of(block_qkv[:, 0], block_qkv[:, 1], live_keys)
    top_score = jnp.max(scores, axis=-1, keepdims=True)
    expo_vals = jnp.exp(scores - top_score)
    row_total = jnp.sum(expo_vals, axis=-1, keepdims=True)
    weights_low = (expo_vals / row_total).astype(jnp.bfloat16)
    context = jnp.einsum(
        "hqk,khd->qhd", weights_low, block_qkv[:, 2], preferred_element_type=jnp.float32
    )
    return (context.astype(jnp.bfloat16), (top_score + jnp.log(row_total))[..., 0])


def attend_back(packed):
    block_qkv, live_keys, log_total, grad_ctx = packed
    queries = block_qkv[:, 0]
    keys_in = block_qkv[:, 1]
    values = block_qkv[:, 2]
    scores = scores_of(queries, keys_in, live_keys)
    weights = jnp.exp(scores - log_total[..., None])
    weights_low = weights.astype(jnp.bfloat16)
    grad_values = jnp.einsum(
        "hqk,qhd->khd", weights_low, grad_ctx, preferred_element_type=jnp.float32
    )
    grad_weights = jnp.einsum("qhd,khd->hqk", grad_ctx, values, preferred_element_type=jnp.float32)
    row_dot = jnp.sum(weights * grad_weights, axis=-1, keepdims=True)
    grad_scores = (weights * (grad_weights - row_dot)).astype(jnp.bfloat16)
    factor = HEAD_DIM ** (-0.5)
    grad_queries = (
        jnp.einsum("hqk,khd->qhd", grad_scores, keys_in, preferred_element_type=jnp.float32)
        * factor
    )
    grad_keys = (
        jnp.einsum("hqk,qhd->khd", grad_scores, queries, preferred_element_type=jnp.float32)
        * factor
    )
    return jnp.stack([grad_queries, grad_keys, grad_values], axis=1).astype(jnp.bfloat16)


def shards(
    hidden_in,
    lengths,
    labels,
    out_cotangent,
    qkv_weight,
    out_weight,
    up_weight,
    down_weight,
    pool_weight,
    class_weight,
    norm_gains,
    biases,
    up_bias,
    class_bias,
):
    pos_local, seq_group, width = hidden_in.shape
    row_count = pos_local * seq_group
    n_seq = lax.axis_size("seq")
    seq_pos = lax.axis_index("seq")
    seq_len = pos_local * n_seq
    local_width = width // n_seq
    head_count = local_width // HEAD_DIM
    group_rows = n_seq * row_count
    is_root = seq_pos == 0
    hidden_rows = hidden_in.reshape(row_count, width)
    zero_bias = jnp.zeros((width,), jnp.float32)
    qkv_full = jnp.dot(
        hidden_rows, qkv_weight, preferred_element_type=jnp.float32
    ) + jnp.concatenate([biases[0], zero_bias, biases[1]])
    qkv_low = qkv_full.astype(jnp.bfloat16).reshape(pos_local, seq_group, 3, n_seq, local_width)
    heads_qkv = lax.all_to_all(qkv_low, "seq", split_axis=3, concat_axis=0, tiled=True)
    qkv_heads = jnp.transpose(
        heads_qkv.reshape(seq_len, seq_group, 3, head_count, HEAD_DIM), (1, 0, 2, 3, 4)
    )
    live_heads = jnp.arange(seq_len)[None, :] < lengths[:, None]
    context_heads, log_totals = lax.map(attend_one, (qkv_heads, live_heads))
    context_rows = jnp.transpose(context_heads, (1, 0, 2, 3)).reshape(group_rows, local_width)
    mix_slice = lax.dynamic_slice_in_dim(out_weight, seq_pos * local_width, local_width, 0)
    mixed = lax.psum_scatter(
        jnp.dot(context_rows, mix_slice, preferred_element_type=jnp.float32),
        "seq",
        scatter_dimension=0,
        tiled=True,
    )
    resid_one = hidden_rows.astype(jnp.float32) + (mixed + biases[2])
    middle, normed_one, scale_one = norm_rows(resid_one, norm_gains[0], biases[3])
    middle_low = middle.astype(jnp.bfloat16)
    pre_act = jnp.dot(middle_low, up_weight, preferred_element_type=jnp.float32) + up_bias
    activated, act_pull = jax.vjp(smooth_act, pre_act)
    act_low = activated.astype(jnp.bfloat16)
    branch = jnp.dot(act_low, down_weight, preferred_element_type=jnp.float32) + biases[4]
    final, normed_two, scale_two = norm_rows(middle + branch, norm_gains[1], biases[5])
    hidden_out = final.astype(jnp.bfloat16)
    local_first = hidden_out.reshape(pos_local, seq_group, width)[0].astype(jnp.float32)
    first_term = jnp.where(is_root, local_first, 0.0)
    first_rows = lax.psum_scatter(first_term, "seq", scatter_dimension=0, tiled=True)
    pool_full = pool_weight.astype(jnp.float32)
    class_full = class_weight.astype(jnp.float32)
    pooled = jnp.tanh(jnp.dot(first_rows, pool_full, precision=highest) + biases[6])
    ramp_logits = jnp.dot(pooled, class_full, precision=highest) + class_bias
    top_logit = jnp.max(ramp_logits, axis=-1, keepdims=True)
    expo_logit = jnp.exp(ramp_logits - top_logit)
    chosen = (jnp.arange(ramp_logits.shape[1])[None, :] == labels[:, None]).astype(jnp.float32)
    grad_logits = expo_logit / jnp.sum(expo_logit, axis=-1, keepdims=True) - chosen
    grad_class_w = jnp.dot(pooled.T, grad_logits, precision=highest)
    class_bias_term = jnp.sum(grad_logits, axis=0)
    grad_pre = jnp.dot(grad_logits, class_full.T, precision=highest) * (1.0 - pooled * pooled)
    grad_pool_w = jnp.dot(first_rows.T, grad_pre, precision=highest)
    pool_bias_term = jnp.sum(grad_pre, axis=0)
    grad_first = jnp.dot(grad_pre, pool_full.T, precision=highest)
    first_back = lax.all_gather(grad_first, "seq", axis=0, tiled=True)
    cot_rows = out_cotangent.astype(jnp.float32)
    cot_rows = cot_rows.at[0].add(jnp.where(is_root, first_back, 0.0))
    grad_final = cot_rows.reshape(row_count, width)
    grad_two, gain_two_grad, shift_two_grad = norm_back(
        grad_final, normed_two, scale_two, norm_gains[1]
    )
    branch_grad = grad_two.astype(jnp.bfloat16)
    down_bias_grad = jnp.sum(branch_grad, axis=0, dtype=jnp.float32)
    grad_down_w = inner_dot(act_low, branch_grad)
    act_grad = trans_dot(branch_grad, down_weight)
    pre_grad = act_pull(act_grad)[0].astype(jnp.bfloat16)
    up_bias_grad = jnp.sum(pre_grad, axis=0, dtype=jnp.float32)
    grad_up_w = inner_dot(middle_low, pre_grad)
    grad_middle = grad_two + trans_dot(pre_grad, up_weight)
    outer_vectors = jnp.stack([gain_two_grad, down_bias_grad, shift_two_grad, pool_bias_term])
    grad_one, gain_one_grad, shift_one_grad = norm_back(
        grad_middle, normed_one, scale_one, norm_gains[0]
    )
    mix_grad = grad_one.astype(jnp.bfloat16)
    out_bias_grad = jnp.sum(mix_grad, axis=0, dtype=jnp.float32)
    piece_rows = lax.all_gather(mix_grad, "seq", axis=0, tiled=True)
    part_ctx = trans_dot(piece_rows, mix_slice)
    mix_acc = inner_dot(context_rows, piece_rows)
    context_grad = part_ctx.astype(jnp.bfloat16)
    grad_out_w = lax.dynamic_update_slice_in_dim(
        jnp.zeros((width, width), jnp.float32), mix_acc, seq_pos * local_width, 0
    )
    ctx_grad_seq = jnp.transpose(
        context_grad.reshape(seq_len, seq_group, head_count, HEAD_DIM), (1, 0, 2, 3)
    )
    qkv_grad_heads = lax.map(attend_back, (qkv_heads, live_heads, log_totals, ctx_grad_seq))
    qkv_grad_pos = jnp.transpose(qkv_grad_heads, (1, 0, 2, 3, 4)).reshape(
        group_rows, 3, 1, local_width
    )
    qkv_grad_back = lax.all_to_all(qkv_grad_pos, "seq", split_axis=0, concat_axis=2, tiled=True)
    qkv_grad = qkv_grad_back.reshape(row_count, 3 * width)
    qkv_sums = jnp.sum(qkv_grad, axis=0, dtype=jnp.float32)
    grad_qkv_w = inner_dot(hidden_rows, qkv_grad)
    grad_in = grad_one + trans_dot(qkv_grad, qkv_weight)
    inner_vectors = jnp.stack(
        [gain_one_grad, qkv_sums[:width], qkv_sums[2 * width :], out_bias_grad, shift_one_grad]
    )
    all_sums = (
        lax.psum_scatter(grad_qkv_w, ("dp", "seq"), scatter_dimension=0, tiled=True),
        lax.psum_scatter(grad_out_w, ("dp", "seq"), scatter_dimension=0, tiled=True),
        lax.psum_scatter(inner_vectors, ("dp", "seq"), scatter_dimension=1, tiled=True),
        lax.psum_scatter(grad_pool_w, ("dp", "seq"), scatter_dimension=0, tiled=True),
        lax.psum_scatter(grad_class_w, ("dp", "seq"), scatter_dimension=0, tiled=True),
        lax.psum_scatter(grad_up_w, ("dp", "seq"), scatter_dimension=0, tiled=True),
        lax.psum_scatter(grad_down_w, ("dp", "seq"), scatter_dimension=0, tiled=True),
        lax.psum_scatter(outer_vectors, ("dp", "seq"), scatter_dimension=1, tiled=True),
        lax.psum_scatter(up_bias_grad, ("dp", "seq"), scatter_dimension=0, tiled=True),
    )
    inner_sums = all_sums[:3]
    outer_sums = all_sums[3:]
    class_bias_sum = lax.psum(class_bias_term, ("dp", "seq"))
    qkv_sum_w, out_sum_w, inner_vec = inner_sums
    pool_sum_w, class_sum_w, up_sum_w, down_sum_w, outer_vec, up_bias_sum = outer_sums
    gains_sum = jnp.stack([inner_vec[0], outer_vec[0]])
    biases_sum = jnp.stack(
        [
            inner_vec[1],
            inner_vec[2],
            inner_vec[3],
            inner_vec[4],
            outer_vec[1],
            outer_vec[2],
            outer_vec[3],
        ]
    )
    return (
        hidden_out.reshape(pos_local, seq_group, width),
        ramp_logits,
        grad_in.reshape(pos_local, seq_group, width),
        qkv_sum_w,
        out_sum_w,
        up_sum_w,
        down_sum_w,
        pool_sum_w,
        class_sum_w,
        gains_sum,
        biases_sum,
        up_bias_sum,
        class_bias_sum,
    )


def solution(mesh):
    placed = (
        P("seq", "dp", None),
        P("dp"),
        P(("dp", "seq")),
        P("seq", "dp", None),
        P(),
        P(),
        P(),
        P(),
        P(),
        P(),
        P(),
        P(),
        P(),
        P(),
    )
    return jax.shard_map(
        shards,
        mesh=mesh,
        in_specs=placed,
        out_specs=(
            P("seq", "dp", None),
            P(("dp", "seq"), None),
            P("seq", "dp", None),
            P(("dp", "seq"), None),
            P(("dp", "seq"), None),
            P(("dp", "seq"), None),
            P(("dp", "seq"), None),
            P(("dp", "seq"), None),
            P(("dp", "seq"), None),
            P(None, ("dp", "seq")),
            P(None, ("dp", "seq")),
            P(("dp", "seq")),
            P(),
        ),
        check_vma=False,
    )
```

profile of v0, /device:TPU:0, one launch (start us, length us, event | category | flops | bytes accessed | tf_op | source)
XLA Modules:
  0.0 1096.5 jit_solution(7411171017334266240)
XLA Ops:
  16.7 12.8 %reshape.238 = bf16[128,8,3,4,192]{4,3,2,1,0:T(4,128)(2,1)} reshape(bf16[1024,2304]{1,0:T(8,128)(2,1)} %add_convert_fusion.1) | data formatting | bytes 9437184 | tf_op jit(solution)/shard_map/reshape | solution.py:122
  29.5 11.1 %copy.75 = bf16[128,8,3,4,192]{0,4,2,1,3:T(8,128)(2,1)} copy(bf16[128,8,3,4,192]{4,3,2,1,0:T(4,128)(2,1)} %reshape.238) | data formatting | bytes 9437184 | tf_op jit(solution)/shard_map/reshape | solution.py:122
  46.6 53.4 %all-to-all-done = bf16[128,8,3,4,192]{0,4,2,1,3:T(8,128)(2,1)} async-done(((bf16[128,8,3,4,192]{0,4,2,1,3:T(8,128)(2,1)}), bf16[128,8,3,4,192]{0,4,2,1,3:T(8,128)(2,1)}, u32[]{:S(2)}, u32[]{:S(2)}) %all-to-all-start) | async-done | bytes 4718624 | tf_op jit(solution)/shard_map/all_to_all | solution.py:123
  100.0 8.8 copy.76
  116.8 39.0 %while.23 = (s32[]{:T(128)}, bf16[8,512,3,64]{1,3,2,0:T(8,128)(2,1)}, f32[8,3,512]{2,1,0:T(4,128)}, bf16[8,512,3,3,64]{1,4,3,2,0:T(8,128)(2,1)}, pred[8,512]{1,0:T(8,128)(4,1)S(1)}, /*index=5*/s32[]{:T(128)}) while((s32[]{:T(128)}, bf16[8,512,3,64]{1,3,2,0:T(8,128)(2,1)}, f32[8,3,512]{2,1,0:T(4,128)}, bf16[8,512,3,3,64]{1,4,3,2,0:T(8,128)(2,1)}, ...), condition=%wide.region_3.4_spmd, body=%wide.region_0.3_spmd.sunk | while | flops 210860544 | bytes 11461213 | solution.py:128
  163.2 8.5 reshape.240
  184.5 95.5 %reduce-scatter.12.cloned.1.call-done = f32[1024,768]{1,0:T(8,128)} async-done(((f32[4096,768]{1,0:T(8,128)}), f32[1024,768]{1,0:T(8,128)}) %reduce-scatter.12.cloned.1.call-update) | async-done | bytes 3145744 | tf_op jit(solution)/shard_map/reduce_scatter | solution.py:131
  283.8 38.1 %multiply_convert_fusion.1 = (bf16[1024,3072]{1,0:T(8,128)(2,1)S(1)}, f32[1024,3072]{1,0:T(8,128)}, f32[1024,3072]{1,0:T(8,128)}) fusion(f32[3072]{0:T(1024)S(1)} %copy-done.28, bf16[768,3072]{1,0:T(8,128)(2,1)} %param.26, f32[1024,768]{1,0:T(8,128)S(1)} %get-tuple-element.231, f32[768]{0:T(1024)S(1)} %get-tuple-element.187, ...), kind=kOutput, calls=%fused_computation.49 | convolution fusion | flops 5043388416 | bytes 39348224 | tf_op jit(solution)/shard_map/dot_general | solution.py:140
  329.8 11.4 %all-reduce = f32[8,768]{1,0:T(8,128)} all-reduce(f32[8,768]{1,0:T(8,128)} %convert_select_fusion), channel_id=3, replica_groups=mesh['dp'=8,'seq'=4] {'seq'}, use_global_device_ids=true, to_apply=%region_9.10.clone | all-reduce | flops 6144 | bytes 49152
  371.3 19.3 %convert_reduce_fusion = (f32[3072]{0:T(1024)}, bf16[1024,3072]{1,0:T(8,128)(2,1)}) fusion(f32[1024,3072]{1,0:T(8,128)} %get-tuple-element.229, bf16[3072,768]{1,0:T(8,128)(2,1)} %param.27, f32[1024,768]{1,0:T(8,128)} %get-tuple-element.227, f32[1024,3072]{1,0:T(8,128)} %get-tuple-element.238, f32[3072]{0:T(1024)S(1)} %copy-done.29), kind=kOutput, calls=%fused_computation.47 | convolution fusion | flops 4886098944 | bytes 39346176 | tf_op jit(solution)/shard_map/dot_general | solution.py:21
  390.7 11.6 %multiply_reduce_fusion.1 = (f32[768]{0:T(1024)}, f32[1024]{0:T(1024)S(1)}, f32[1024]{0:T(1024)S(1)}, f32[768]{0:T(1024)}, f32[1024,768]{1,0:T(8,128)S(1)}) fusion(f32[1024,768]{1,0:T(8,128)} %copy-done.2, f32[1024]{0:T(1024)S(1)} %add_rsqrt_fusion.1, f32[1024]{0:T(1024)S(1)} %broadcast_multiply_fusion.5, f32[768]{0:T(1024)S(1)} %copy-done.15, ...), kind=kOutput, calls=%fused_computation.72 | convolution fusion | flops 4839698432 | bytes 20472832 | tf_op jit(solution)/shard_map/dot_general | solution.py:21
  410.0 11.0 %fusion.54 = f32[768,3072]{1,0:T(8,128)} fusion(bf16[1024,3072]{1,0:T(8,128)(2,1)} %get-tuple-element.247, f32[1024,768]{1,0:T(8,128)} %copy-done.2, f32[768]{0:T(1024)S(1)} %copy-done.19, f32[768]{0:T(1024)S(1)} %copy-done.15, f32[1024]{0:T(1024)S(1)} %add_rsqrt_fusion.1, f32[1024]{0:T(1024)S(1)} %broadcast_multiply_fusion.5), kind=kOutput, calls=%fused_computation.144 | convolution fusion | flops 4835770368 | bytes 18888704 | tf_op jit(solution)/shard_map/dot_general | solution.py:15
  421.1 10.7 fusion.51
  431.9 21.4 %all-gather.3.cloned.1.call-done = bf16[4096,768]{1,0:T(8,128)(2,1)} async-done(((bf16[1024,768]{1,0:T(8,128)(2,1)}), bf16[4096,768]{1,0:T(8,128)(2,1)}) %all-gather.3.cloned.1.call-update) | async-done | bytes 6291472 | tf_op jit(solution)/shard_map/all_gather | solution.py:184
  463.3 8.6 reshape.244
  478.6 70.0 %while.24 = (s32[]{:T(128)}, bf16[8,512,3,3,64]{1,4,3,2,0:T(8,128)(2,1)}, bf16[8,512,3,3,64]{1,4,3,2,0:T(8,128)(2,1)}, pred[8,512]{1,0:T(8,128)(4,1)S(1)}, f32[8...) while((s32[]{:T(128)}, bf16[8,512,3,3,64]{1,4,3,2,0:T(8,128)(2,1)}, ...), condition=%wide.region_18.19_spmd, body=%wide.region_16.18_spmd.sunk | while | flops 512653824 | bytes 27952748 | solution.py:194
  548.5 20.0 %copy.91 = bf16[512,8,3,3,64]{4,3,2,1,0:T(4,128)(2,1)} copy(bf16[512,8,3,3,64]{0,4,3,2,1:T(8,128)(2,1)} %bitcast.178) | data formatting | bytes 9437184 | tf_op jit(solution)/shard_map/reshape | solution.py:195
  568.6 30.5 %reshape.254 = bf16[4096,3,1,192]{3,1,2,0:T(4,128)(2,1)} reshape(bf16[512,8,3,3,64]{4,3,2,1,0:T(4,128)(2,1)} %copy.91) | data formatting | bytes 9437184 | tf_op jit(solution)/shard_map/reshape | solution.py:195
  612.5 108.7 %all-to-all-done.1 = bf16[4096,3,1,192]{3,1,2,0:T(4,128)(2,1)} async-done(((bf16[4096,3,1,192]{3,1,2,0:T(4,128)(2,1)}), bf16[4096,3,1,192]{3,1,2,0:T(4,128)(2,1)}, u32[]{:S(2)}, u32[]{:S(2)}) %all-to-all-start.1) | async-done | bytes 4718624 | tf_op jit(solution)/shard_map/all_to_all | solution.py:198
  721.2 14.0 %copy.92 = bf16[4,1024,3,1,192]{1,0,4,2,3:T(4,128)(2,1)} copy(bf16[4,1024,3,1,192]{4,2,1,0,3:T(4,128)(2,1)} %bitcast.29) | data formatting | bytes 9437184 | tf_op jit(solution)/shard_map/all_to_all | solution.py:198
  777.9 42.3 %all-reduce.5 = (f32[768,3]{0,1:T(4,128)}, f32[4,768]{1,0:T(4,128)}, f32[5,768]{1,0:T(8,128)}, f32[3072]{0:T(1024)}, f32[3]{0:T(128)}) all-reduce(f32[768,3]{0,1:T(4,128)} %fusion.66, f32[4,768]{1,0:T(4,128)S(1)} %copy-done.20, f32[5,768]{1,0:T(8,128)} %stack.57, ...), channel_id=9, replica_groups=mesh['dp'=8,'seq'=4] {'dp','seq'}, use_global_device_ids=true, to_apply=%region_24.25.clone | all-reduce | flops 12291 | bytes 98328
  833.7 26.4 %reduce-scatter.18.cloned.1.call-done = f32[96,768]{1,0:T(8,128)} async-done(((f32[3072,768]{1,0:T(8,128)}), f32[96,768]{1,0:T(8,128)}) %reduce-scatter.18.cloned.1.call-update) | async-done | bytes 294928 | tf_op jit(solution)/shard_map/reduce_scatter | solution.py:213
  860.1 104.6 %reduce-scatter.14.cloned.1.call-done = f32[24,768]{1,0:T(8,128)} async-done(((f32[768,768]{1,0:T(8,128)}), f32[24,768]{1,0:T(8,128)}) %reduce-scatter.14.cloned.1.call-update) | async-done | bytes 73744 | tf_op jit(solution)/shard_map/reduce_scatter | solution.py:208
  964.7 124.5 %reduce-scatter.22.cloned.1.call-done = f32[24,2304]{1,0:T(8,128)} async-done(((f32[768,2304]{1,0:T(8,128)}), f32[24,2304]{1,0:T(8,128)}) %reduce-scatter.22.cloned.1.call-update) | async-done | bytes 221200
  (294 shorter events, 287.2 us)
Async XLA Ops:
  8.9 313.0 %copy-start.14 = (f32[768]{0:T(1024)}, f32[768]{0:T(1024)S(1)}, u32[]{:S(2)}) copy-start(f32[768]{0:T(1024)S(1)} %get-tuple-element.248) | copy-start | bytes 9220
  8.9 313.0 %copy-start.18 = (f32[768]{0:T(1024)}, f32[768]{0:T(1024)S(1)}, u32[]{:S(2)}) copy-start(f32[768]{0:T(1024)S(1)} %get-tuple-element.187) | copy-start | bytes 9220
  40.6 59.4 %all-to-all-start = ((bf16[128,8,3,4,192]{0,4,2,1,3:T(8,128)(2,1)}), bf16[128,8,3,4,192]{0,4,2,1,3:T(8,128)(2,1)}, u32[]{:S(2)}, u32[]{:S(2)}) async-start(bf16[128,8,3,4,192]{0,4,2,1,3:T(8,128)(2,1)} %copy.75), calls=%async_computation | async-start | bytes 9437184 | tf_op jit(solution)/shard_map/all_to_all | solution.py:123
  45.5 234.5 %reduce-scatter.12.cloned.1.call-start = ((), (), s32[]{:S(2)}) async-start(), calls=%async_computation.8 | async-start | bytes 15728640 | tf_op jit(solution)/shard_map/reduce_scatter | solution.py:131
  155.8 15.9 %copy-start.8 = (pred[8,512]{1,0:T(8,128)(4,1)}, pred[8,512]{1,0:T(8,128)(4,1)S(1)}, u32[]{:S(2)}) copy-start(pred[8,512]{1,0:T(8,128)(4,1)S(1)} %get-tuple-element.391) | copy-start | bytes 12292
  179.7 273.6 %all-gather.3.cloned.1.call-start = ((), (), s32[]{:S(2)}) async-start(), calls=%async_computation.9 | async-start | bytes 7864320 | tf_op jit(solution)/shard_map/all_gather | solution.py:184
  280.1 41.8 %slice-start = ((s8[4718592]{0:T(1024)(128)(4,1)}), s8[4194304]{0:T(1024)(128)(4,1)S(1)}, s32[]{:S(2)}) async-start(s8[4718592]{0:T(1024)(128)(4,1)} %bitcast.180), calls=%async_computation.15 | async-start | bytes 8388608
  283.1 38.8 %copy-start.2 = (f32[1024,768]{1,0:T(8,128)}, f32[1024,768]{1,0:T(8,128)S(1)}, u32[]{:S(2)}) copy-start(f32[1024,768]{1,0:T(8,128)S(1)} %get-tuple-element.231) | copy-start | bytes 9437188
  283.8 38.1 %copy-start.25 = (f32[768]{0:T(1024)S(1)}, f32[768]{0:T(1024)}, u32[]{:S(2)}) copy-start(f32[768]{0:T(1024)} %get-tuple-element.186) | copy-start | bytes 9220
  283.8 38.1 %slice-start.1 = ((s8[4718592]{0:T(1024)(128)(4,1)}), s8[524288]{0:T(1024)(128)(4,1)S(1)}, s32[]{:S(2)}) async-start(s8[4718592]{0:T(1024)(128)(4,1)} %bitcast.180), calls=%async_computation.16 | async-start | bytes 1048576
  327.5 38.5 %copy-start.12 = (f32[1024]{0:T(1024)}, f32[1024]{0:T(1024)S(1)}, u32[]{:S(2)}) copy-start(f32[1024]{0:T(1024)S(1)} %broadcast_multiply_fusion.4) | copy-start | bytes 12292
  371.3 19.3 %copy-start.15 = (f32[768]{0:T(1024)S(1)}, f32[768]{0:T(1024)}, u32[]{:S(2)}) copy-start(f32[768]{0:T(1024)} %copy-done.14) | copy-start | bytes 9220
  390.7 11.6 %copy-start.3 = (f32[1024,768]{1,0:T(8,128)S(1)}, f32[1024,768]{1,0:T(8,128)}, u32[]{:S(2)}) copy-start(f32[1024,768]{1,0:T(8,128)} %copy-done.2) | copy-start | bytes 9437188
  405.6 428.1 %reduce-scatter.20.cloned.1.call-start = ((), (), s32[]{:S(2)}) async-start(), calls=%async_computation.13 | async-start | bytes 2433024 | tf_op jit(solution)/shard_map/reduce_scatter | solution.py:210
  410.0 423.7 %reduce-scatter.16.cloned.1.call-start = ((), (), s32[]{:S(2)}) async-start(), calls=%async_computation.11 | async-start | bytes 9732096 | tf_op jit(solution)/shard_map/reduce_scatter | solution.py:212
  421.1 439.0 %reduce-scatter.18.cloned.1.call-start = ((), (), s32[]{:S(2)}) async-start(), calls=%async_computation.12 | async-start | bytes 9732096 | tf_op jit(solution)/shard_map/reduce_scatter | solution.py:213
  599.1 122.1 %all-to-all-start.1 = ((bf16[4096,3,1,192]{3,1,2,0:T(4,128)(2,1)}), bf16[4096,3,1,192]{3,1,2,0:T(4,128)(2,1)}, u32[]{:S(2)}, u32[]{:S(2)}) async-start(bf16[4096,3,1,192]{3,1,2,0:T(4,128)(2,1)} %reshape.254), calls=%async_computation.2 | async-start | bytes 16777216 | tf_op jit(solution)/shard_map/all_to_all | solution.py:198
  604.8 359.9 %reduce-scatter.14.cloned.1.call-start = ((), (), s32[]{:S(2)}) async-start(), calls=%async_computation.10 | async-start | bytes 2433024 | tf_op jit(solution)/shard_map/reduce_scatter | solution.py:208
  612.5 476.7 %reduce-scatter.22.cloned.1.call-start = ((), (), s32[]{:S(2)}) async-start(), calls=%async_computation.14 | async-start | bytes 7299072
  755.9 8.7 copy-start.11
  755.9 8.7 copy-start.13
  755.9 8.7 copy-start.17
  755.9 8.7 copy-start.22
  768.2 9.7 copy-start.20
  (19 other events, 64.7 us)
Sparse Core Ops, SparseCore 0:
  179.8 100.2 reduce-scatter.11
  405.7 47.5 all-gather.2
  459.2 99.0 reduce-scatter.19
  565.6 152.6 reduce-scatter.15
  724.6 135.4 reduce-scatter.17
  866.7 98.0 reduce-scatter.13
  971.0 118.1 reduce-scatter.21
where the time goes:
time: 1110 us; the launch traced here: 1100 us
  waiting for transfers between devices  535 us (48%)
  matrix products  210 us (19%)
  local copies, waits for them, and re-layouts  204 us (18%)
  other arithmetic  61.9 us (6%)
  blocking collectives  59 us (5%)
  between operations  15.6 us (1%)
  starting transfers between devices  11.4 us (1%)
    unnamed x8, waiting for transfers between devices  125 us
    all_to_all x1, waiting for transfers between devices, shards(): lax.all_to_all(qkv_grad_pos, 'seq', split_axis=0, concat_axis=2, tiled=True)  109 us
    reduce_scatter x1, waiting for transfers between devices, shards(): lax.psum_scatter(grad_out_w, ('dp', 'seq'), scatter_dimension=0, tiled=True)  105 us
    reduce_scatter x1, waiting for transfers between devices, shards(): lax.psum_scatter(jnp.dot(context_rows, mix_slice, preferred_element_type=...  95.5 us
    unnamed x2, blocking collectives  53.8 us
    all_to_all x1, waiting for transfers between devices, shards(): lax.all_to_all(qkv_low, 'seq', split_axis=3, concat_axis=0, tiled=True)  53.4 us
    reshape x2, local copies, waits for them, and re-layouts, shards(): jnp.transpose(qkv_grad_heads, (1, 0, 2, 3, 4))  50.5 us
    dot_general x4, matrix products, trans_dot(): lax.dot_general(left_in, right_in, (((1,), (1,)), ((), ())), preferred_el...  45.1 us
  transfers between devices with their start and end apart: 9, of which 7 were waited for; matrix products, arithmetic and copies ran while one was open for 23% of the time, Pallas kernels for 0%

commit v1 on v0

v1 whole, which is shorter than its diff:
```python
import functools

import jax
import jax.numpy as jnp
from jax import lax
from jax.experimental import pallas as pl
from jax.experimental.pallas import tpu as pltpu
from jax.sharding import PartitionSpec as P

HEAD_DIM = 64
PAIR = 2 * HEAD_DIM
REC = 8

eps = 1e-12
neg_big = -1e30
highest = lax.Precision.HIGHEST
f32 = jnp.float32
bf16 = jnp.bfloat16
MIB = 1 << 20

ERF_P = 0.3275911
ERF_A = (0.254829592, -0.284496736, 1.421413741, -1.453152027, 1.061405429)


def nn(left, right):
    return lax.dot_general(left, right, (((1,), (0,)), ((), ())), preferred_element_type=f32)


def nt(left, right):
    return lax.dot_general(left, right, (((1,), (1,)), ((), ())), preferred_element_type=f32)


def tn(left, right):
    return lax.dot_general(left, right, (((0,), (0,)), ((), ())), preferred_element_type=f32)


def params(limit=56):
    return pltpu.CompilerParams(vmem_limit_bytes=limit * MIB)


def cost(flops, nbytes, trans=0):
    return pl.CostEstimate(flops=int(flops), bytes_accessed=int(nbytes), transcendentals=int(trans))


def smem():
    return pl.BlockSpec(memory_space=pltpu.SMEM)


def whole(shape):
    return pl.BlockSpec(shape, lambda *_: (0,) * len(shape))


def three_parts(value):
    hi = value.astype(bf16)
    rest = value - hi.astype(f32)
    mid = rest.astype(bf16)
    low = (rest - mid.astype(f32)).astype(bf16)
    return jnp.concatenate([hi, mid, low], axis=0)


def fine_dot(dot, value, weight):
    rows = value.shape[0]
    parts = dot(jnp.concatenate([three_parts(value)], axis=0), weight)
    return parts[:rows] + parts[rows : 2 * rows] + parts[2 * rows :]


def split_kernel(info, rows, *outs):
    chunks = len(outs)
    per, span, _ = outs[0].shape
    group = chunks * per
    block = 16 * group
    own = info[0]
    dest = lax.broadcasted_iota(jnp.int32, (block, block), 0)
    source = lax.broadcasted_iota(jnp.int32, (block, block), 1)
    chunk = dest // (16 * per)
    wanted = (dest % 16) * group + per * (chunk ^ own) + (dest // 16) % per
    perm = jnp.where(source == wanted, 1.0, 0.0).astype(bf16)
    for b in range(span // 16):
        moved = nn(perm, rows[b * block : (b + 1) * block, :]).astype(bf16)
        for c in range(chunks):
            for q in range(per):
                at = (c * per + q) * 16
                outs[c][q, b * 16 : (b + 1) * 16, :] = moved[at : at + 16]


def split_rows(info, rows, positions, group, chunks):
    width = rows.shape[1]
    per = group // chunks
    steps = 4
    span = positions // steps
    return pl.pallas_call(
        split_kernel,
        grid=(steps,),
        in_specs=[smem(), pl.BlockSpec((span * group, width), lambda i: (i, 0))],
        out_specs=[pl.BlockSpec((per, span, width), lambda i: (0, i, 0))] * chunks,
        out_shape=[jax.ShapeDtypeStruct((per, positions, width), bf16)] * chunks,
        compiler_params=params(),
        cost_estimate=cost(2 * rows.size * 16 * group, 4 * rows.size),
        name="split_rows",
    )(info, rows)


def merge_kernel(info, *refs):
    ins, out = refs[:-1], refs[-1]
    chunks = len(ins)
    per, span, _ = ins[0].shape
    group = chunks * per
    block = 16 * group
    own = info[0]
    dest = lax.broadcasted_iota(jnp.int32, (block, block), 0)
    source = lax.broadcasted_iota(jnp.int32, (block, block), 1)
    seq = dest % group
    wanted = (((seq // per) ^ own) * per + seq % per) * 16 + dest // group
    perm = jnp.where(source == wanted, 1.0, 0.0).astype(bf16)
    for b in range(span // 16):
        rows = jnp.concatenate(
            [ins[c][q, b * 16 : (b + 1) * 16, :] for c in range(chunks) for q in range(per)], axis=0
        )
        out[b * block : (b + 1) * block, :] = nn(perm, rows).astype(out.dtype)


def merge_rows(info, parts, dtype):
    chunks = len(parts)
    per, positions, width = parts[0].shape
    group = per * chunks
    steps = 4
    span = positions // steps
    return pl.pallas_call(
        merge_kernel,
        grid=(steps,),
        in_specs=[smem()] + [pl.BlockSpec((per, span, width), lambda i: (0, i, 0))] * chunks,
        out_specs=pl.BlockSpec((span * group, width), lambda i: (i, 0)),
        out_shape=jax.ShapeDtypeStruct((positions * group, width), dtype),
        compiler_params=params(),
        cost_estimate=cost(2 * positions * group * width * 16 * group, 6 * positions * group * width),
        name="merge_rows",
    )(info, *parts)


def exchange(parts):
    size = lax.axis_size("seq")
    return [parts[0]] + [
        lax.ppermute(parts[c], "seq", [(i, i ^ c) for i in range(size)]) for c in range(1, size)
    ]


def row_stats(resid):
    mean = jnp.mean(resid, axis=-1, keepdims=True)
    centred = resid - mean
    scale = lax.rsqrt(jnp.mean(centred * centred, axis=-1, keepdims=True) + eps)
    return centred * scale, scale


def attend_kernel(info, *refs):
    chunks = len(refs) - 10
    parts = refs[:chunks]
    qkv_w, out_w, biases, x_out, qkv, context, lse, normed, scale, stats = refs[chunks:]
    width = out_w.shape[0]
    span = parts[0].shape[1]
    length = chunks * span
    pairs = width // PAIR
    own = info[0]
    live_len = info[1 + pl.program_id(0)]
    x_out[...] = jnp.concatenate([part[0] for part in parts], axis=0)
    for third in range(3):
        cols = slice(third * width, (third + 1) * width)
        block = nn(x_out[...], qkv_w[:, cols])
        if third == 0:
            block = block + biases[0:1, :]
        elif third == 2:
            block = block + biases[1:2, :]
        qkv[:, cols] = block.astype(bf16)
    lane = lax.broadcasted_iota(jnp.int32, (length, PAIR), 1)
    row = lax.broadcasted_iota(jnp.int32, (length, PAIR), 0)
    pos = ((row // span) ^ own) * span + row % span
    key_ext = jnp.where((lane == 0) & (pos >= live_len), neg_big, 0.0).astype(bf16)
    query_ext = jnp.where(lane == 0, 1.0, 0.0).astype(bf16)
    low_half = lane < HEAD_DIM
    masks = [jnp.where(low_half, 1.0, 0.0).astype(bf16), jnp.where(low_half, 0.0, 1.0).astype(bf16)]
    stats[...] = jnp.zeros_like(stats)

    def one_pair(i, carry):
        start = pl.multiple_of(i * PAIR, PAIR)
        queries = qkv[:, pl.ds(start, PAIR)] * bf16(HEAD_DIM**-0.5)
        keys = jnp.concatenate([qkv[:, pl.ds(start + width, PAIR)], key_ext], axis=1)
        values = qkv[:, pl.ds(start + 2 * width, PAIR)]
        total = None
        tops = []
        for head in range(2):
            scores = nt(jnp.concatenate([queries * masks[head], query_ext], axis=1), keys)
            top = jnp.max(scores, axis=1, keepdims=True)
            weights = jnp.exp(scores - top).astype(bf16)
            part = nn(weights, jnp.concatenate([values * masks[head], masks[head]], axis=1))
            total = part if total is None else total + part
            tops.append(top)
        row_total = total[:, PAIR:]
        context[:, pl.ds(start, PAIR)] = (total[:, :PAIR] / row_total).astype(bf16)
        log_total = jnp.where(low_half, tops[0], tops[1]) + jnp.log(row_total)
        swapped = pltpu.roll(log_total, HEAD_DIM, 1)
        stats[...] = jnp.where(
            lane == 2 * i, log_total, jnp.where(lane == 2 * i + 1, swapped, stats[...])
        )
        return carry

    lax.fori_loop(0, pairs, one_pair, 0)
    lse[0] = jnp.transpose(stats[...])[: lse.shape[1], :]
    resid = x_out[...].astype(f32) + (nn(context[...], out_w[...]) + biases[2:3, :])
    n_one, q_one = row_stats(resid)
    normed[...] = n_one
    scale[...] = q_one


def attend(info, parts, qkv_w, out_w, biases):
    chunks = len(parts)
    per, span, width = parts[0].shape
    length = chunks * span
    rows = per * length
    heads = width // HEAD_DIM
    head_rows = -(-heads // 8) * 8
    by_seq = lambda i: (i, 0)
    return pl.pallas_call(
        attend_kernel,
        grid=(per,),
        in_specs=[smem()]
        + [pl.BlockSpec((1, span, width), lambda i: (i, 0, 0))] * chunks
        + [whole(qkv_w.shape), whole(out_w.shape), whole(biases.shape)],
        out_specs=[
            pl.BlockSpec((length, width), by_seq),
            pl.BlockSpec((length, 3 * width), by_seq),
            pl.BlockSpec((length, width), by_seq),
            pl.BlockSpec((1, head_rows, length), lambda i: (i, 0, 0)),
            pl.BlockSpec((length, width), by_seq),
            pl.BlockSpec((length, 1), by_seq),
        ],
        out_shape=[
            jax.ShapeDtypeStruct((rows, width), bf16),
            jax.ShapeDtypeStruct((rows, 3 * width), bf16),
            jax.ShapeDtypeStruct((rows, width), bf16),
            jax.ShapeDtypeStruct((per, head_rows, length), f32),
            jax.ShapeDtypeStruct((rows, width), f32),
            jax.ShapeDtypeStruct((rows, 1), f32),
        ],
        scratch_shapes=[pltpu.VMEM((length, PAIR), f32)],
        compiler_params=params(),
        cost_estimate=cost(
            8 * rows * width * width + 8 * rows * length * width, 20 * rows * width + 8 * width * width,
            rows * length * heads,
        ),
        name="attend",
    )(info, *parts, qkv_w, out_w, biases)


def gelu_pair(x):
    size = jnp.abs(x)
    denom = 1.0 + (ERF_P * 2**-0.5) * size
    t = 1.0 / denom
    bell = jnp.exp(-0.5 * (x * x))
    poly = ERF_A[4]
    for coef in ERF_A[3::-1]:
        poly = poly * t + coef
    tail = (0.5 * poly) * t * bell
    cdf = jnp.where(x >= 0.0, 1.0 - tail, tail)
    return x * cdf, cdf + x * bell * (0.5 / jnp.pi) ** 0.5


def feed_kernel(info, normed, up_w, up_b, down_w, gains, biases, pool_w, class_w, class_b, *outs):
    middle_out, act, slope, normed_two, scale_two, record = outs[:6]
    finals = outs[6:]
    chunks = len(finals)
    span = finals[0].shape[1]
    own = info[0]
    middle = normed[...] * gains[0:1, :] + biases[3:4, :]
    middle_out[...] = middle.astype(bf16)
    hidden = up_w.shape[1]
    tile = 256
    for j in range(hidden // tile):
        cols = slice(j * tile, (j + 1) * tile)
        pre = nn(middle_out[...], up_w[:, cols]) + up_b[:, cols]
        value, grad = gelu_pair(pre)
        act[:, cols] = value.astype(bf16)
        slope[:, cols] = grad.astype(bf16)
    branch = nn(act[...], down_w[...]) + biases[4:5, :]
    middle = normed[...] * gains[0:1, :] + biases[3:4, :]
    n_two, q_two = row_stats(middle + branch)
    normed_two[...] = n_two
    scale_two[...] = q_two
    for c in range(chunks):
        rows = slice(c * span, (c + 1) * span)
        finals[c][0] = (normed_two[rows, :] * gains[1:2, :] + biases[5:6, :]).astype(bf16)
    label = info[1 + pl.num_programs(0) + pl.program_id(0)]
    start = pl.multiple_of(own * span, 8)
    first = (normed_two[pl.ds(start, REC), :] * gains[1:2, :] + biases[5:6, :]).astype(bf16)
    pooled = jnp.tanh(nn(first, pool_w[...]) + biases[6:7, :])
    logits = fine_dot(nt, pooled, class_w[...]) + class_b[...]
    expo = jnp.exp(logits - jnp.max(logits, axis=1, keepdims=True))
    lane = lax.broadcasted_iota(jnp.int32, logits.shape, 1)
    g_logits = expo / jnp.sum(expo, axis=1, keepdims=True) - jnp.where(lane == label, 1.0, 0.0)
    g_pre = fine_dot(nn, g_logits, class_w[...]) * (1.0 - pooled * pooled)
    g_first = fine_dot(nt, g_pre, pool_w[...])
    record[...] = jnp.zeros_like(record)
    record[0:1, :] = first.astype(f32)[0:1, :]
    record[1:2, :] = g_pre[0:1, :]
    record[2:3, :] = pooled[0:1, :]
    record[3:4, :] = g_first[0:1, :]
    lanes = logits.shape[1]
    record[4:5, :lanes] = logits[0:1, :]
    record[5:6, :lanes] = g_logits[0:1, :]


def feed(info, normed, up_w, up_b, down_w, gains, biases, pool_w, class_w, class_b, per, chunks):
    rows, width = normed.shape
    length = rows // per
    span = length // chunks
    hidden = up_w.shape[1]
    by_seq = lambda i: (i, 0)
    consts = (up_w, up_b, down_w, gains, biases, pool_w, class_w, class_b)
    return pl.pallas_call(
        feed_kernel,
        grid=(per,),
        in_specs=[smem(), pl.BlockSpec((length, width), by_seq)] + [whole(a.shape) for a in consts],
        out_specs=[
            pl.BlockSpec((length, width), by_seq),
            pl.BlockSpec((length, hidden), by_seq),
            pl.BlockSpec((length, hidden), by_seq),
            pl.BlockSpec((length, width), by_seq),
            pl.BlockSpec((length, 1), by_seq),
            pl.BlockSpec((REC, width), by_seq),
        ]
        + [pl.BlockSpec((1, span, width), lambda i: (i, 0, 0))] * chunks,
        out_shape=[
            jax.ShapeDtypeStruct((rows, width), bf16),
            jax.ShapeDtypeStruct((rows, hidden), bf16),
            jax.ShapeDtypeStruct((rows, hidden), bf16),
            jax.ShapeDtypeStruct((rows, width), f32),
            jax.ShapeDtypeStruct((rows, 1), f32),
            jax.ShapeDtypeStruct((per * REC, width), f32),
        ]
        + [jax.ShapeDtypeStruct((per, span, width), bf16)] * chunks,
        compiler_params=params(),
        cost_estimate=cost(4 * rows * width * hidden, 4 * rows * hidden + 4 * width * hidden + 12 * rows * width),
        name="feed",
    )(info, normed, *consts)


def norm_back(upper, normed, scale, gain):
    scaled = upper * gain
    mean_part = jnp.mean(scaled, axis=-1, keepdims=True)
    proj_part = jnp.mean(scaled * normed, axis=-1, keepdims=True)
    return scale * (scaled - mean_part - normed * proj_part)


def col_sum(values):
    return jnp.sum(values, axis=0, keepdims=True)


def feed_back_kernel(info, *refs):
    chunks = len(refs) - 17
    cots = refs[:chunks]
    record, n_two, q_two, slope, down_w, up_w, out_w, n_one, q_one, gains = refs[chunks : chunks + 10]
    branch_grad, pre_grad, grad_one, mix_grad, context_grad, sums, up_sums = refs[chunks + 10 :]
    span = cots[0].shape[1]
    length = chunks * span
    own = info[0]

    @pl.when(pl.program_id(0) == 0)
    def _():
        sums[...] = jnp.zeros_like(sums)
        up_sums[...] = jnp.zeros_like(up_sums)

    cot = jnp.concatenate([part[0] for part in cots], axis=0).astype(f32)
    row = lax.broadcasted_iota(jnp.int32, (length, 1), 0)
    g_final = cot + jnp.where(row == own * span, record[3:4, :], 0.0)
    normed = n_two[...]
    sums[0:1, :] += col_sum(g_final * normed)
    sums[2:3, :] += col_sum(g_final)
    g_two = norm_back(g_final, normed, q_two[...], gains[1:2, :])
    branch_grad[...] = g_two.astype(bf16)
    sums[1:2, :] += col_sum(branch_grad[...].astype(f32))
    grad_one[...] = g_two
    hidden = up_w.shape[1]
    tile = 256
    for j in range(hidden // tile):
        cols = slice(j * tile, (j + 1) * tile)
        pre = nt(branch_grad[...], down_w[cols, :]) * slope[:, cols].astype(f32)
        low = pre.astype(bf16)
        pre_grad[:, cols] = low
        up_sums[:, cols] += col_sum(low.astype(f32))
    g_middle = grad_one[...] + nt(pre_grad[...], up_w[...])
    normed = n_one[...]
    sums[3:4, :] += col_sum(g_middle * normed)
    sums[5:6, :] += col_sum(g_middle)
    g_one = norm_back(g_middle, normed, q_one[...], gains[0:1, :])
    grad_one[...] = g_one
    mix_grad[...] = g_one.astype(bf16)
    sums[4:5, :] += col_sum(mix_grad[...].astype(f32))
    context_grad[...] = nt(mix_grad[...], out_w[...]).astype(bf16)


def feed_back(info, cots, record, n_two, q_two, slope, down_w, up_w, out_w, n_one, q_one, gains):
    chunks = len(cots)
    per, span, width = cots[0].shape
    rows, hidden = slope.shape
    length = rows // per
    by_seq = lambda i: (i, 0)
    row_block = pl.BlockSpec((length, width), by_seq)
    wide_block = pl.BlockSpec((length, hidden), by_seq)
    thin_block = pl.BlockSpec((length, 1), by_seq)
    return pl.pallas_call(
        feed_back_kernel,
        grid=(per,),
        in_specs=[smem()]
        + [pl.BlockSpec((1, span, width), lambda i: (i, 0, 0))] * chunks
        + [
            pl.BlockSpec((REC, width), by_seq),
            row_block,
            thin_block,
            wide_block,
            whole(down_w.shape),
            whole(up_w.shape),
            whole(out_w.shape),
            row_block,
            thin_block,
            whole(gains.shape),
        ],
        out_specs=[row_block, wide_block, row_block, row_block, row_block, whole((8, width)), whole((1, hidden))],
        out_shape=[
            jax.ShapeDtypeStruct((rows, width), bf16),
            jax.ShapeDtypeStruct((rows, hidden), bf16),
            jax.ShapeDtypeStruct((rows, width), f32),
            jax.ShapeDtypeStruct((rows, width), bf16),
            jax.ShapeDtypeStruct((rows, width), bf16),
            jax.ShapeDtypeStruct((8, width), f32),
            jax.ShapeDtypeStruct((1, hidden), f32),
        ],
        compiler_params=params(),
        cost_estimate=cost(
            4 * rows * width * hidden + 2 * rows * width * width,
            4 * rows * hidden + 4 * width * hidden + 20 * rows * width,
        ),
        name="feed_back",
    )(info, *cots, record, n_two, q_two, slope, down_w, up_w, out_w, n_one, q_one, gains)


def attend_back_kernel(info, queries_in, keys_in, values_in, context_grad, context, lse, grads, sums, *, chunks):
    length = queries_in.shape[0]
    span = length // chunks
    own = info[0]
    i = pl.program_id(0)
    live_len = info[1 + pl.program_id(1)]
    factor = HEAD_DIM**-0.5
    lane = lax.broadcasted_iota(jnp.int32, (length, PAIR), 1)
    row = lax.broadcasted_iota(jnp.int32, (length, PAIR), 0)
    pos = ((row // span) ^ own) * span + row % span
    key_ext = jnp.where((lane == 0) & (pos >= live_len), neg_big, 0.0).astype(bf16)
    query_ext = jnp.where(lane == 0, 1.0, 0.0).astype(bf16)
    low_half = lane < HEAD_DIM
    masks = [jnp.where(low_half, 1.0, 0.0).astype(bf16), jnp.where(low_half, 0.0, 1.0).astype(bf16)]
    queries = queries_in[...] * bf16(factor)
    keys = jnp.concatenate([keys_in[...], key_ext], axis=1)
    values = values_in[...]
    ctx_grad = context_grad[...]
    product = ctx_grad.astype(f32) * context[...].astype(f32)
    picks = jnp.where(
        lax.broadcasted_iota(jnp.int32, (8, PAIR), 1) // HEAD_DIM
        == lax.broadcasted_iota(jnp.int32, (8, PAIR), 0),
        1.0,
        0.0,
    ).astype(bf16)
    high = product.astype(bf16)
    low = (product - high.astype(f32)).astype(bf16)
    row_dots = nt(picks, high) + nt(picks, low)
    block = length // 2
    g_queries = None
    g_keys = [None, None]
    g_values = [None, None]
    for head in range(2):
        masked_q = queries * masks[head]
        long_q = jnp.concatenate([masked_q, query_ext], axis=1)
        masked_g = ctx_grad * masks[head]
        log_total = lse[0, pl.ds(2 * i + head, 1), :]
        row_dot = row_dots[head : head + 1, :]
        for c in range(2):
            rows = slice(c * block, (c + 1) * block)
            weights = jnp.exp(nt(keys[rows], long_q) - log_total)
            part = nn(weights.astype(bf16), masked_g)
            g_values[c] = part if g_values[c] is None else g_values[c] + part
            g_scores = (weights * (nt(values[rows], masked_g) - row_dot)).astype(bf16)
            part = nn(g_scores, masked_q)
            g_keys[c] = part if g_keys[c] is None else g_keys[c] + part
            part = tn(g_scores, keys_in[rows, :] * masks[head][rows])
            g_queries = part if g_queries is None else g_queries + part
    grads[0] = (g_queries * factor).astype(bf16)
    for c in range(2):
        rows = slice(c * block, (c + 1) * block)
        grads[1, rows, :] = g_keys[c].astype(bf16)
        grads[2, rows, :] = g_values[c].astype(bf16)

    @pl.when(pl.program_id(1) == 0)
    def _():
        sums[...] = jnp.zeros_like(sums)

    sums[0:1, :] += col_sum(grads[0].astype(f32))
    sums[1:2, :] += col_sum(grads[2].astype(f32))


def attend_back(info, qkv, context_grad, context, lse, chunks):
    rows, width = context.shape
    per, head_rows, length = lse.shape
    pairs = width // PAIR
    spec = lambda third: pl.BlockSpec((length, PAIR), lambda i, q: (q, third * pairs + i))
    return pl.pallas_call(
        functools.partial(attend_back_kernel, chunks=chunks),
        grid=(pairs, per),
        in_specs=[
            smem(),
            spec(0),
            spec(1),
            spec(2),
            spec(0),
            spec(0),
            pl.BlockSpec((1, head_rows, length), lambda i, q: (q, 0, 0)),
        ],
        out_specs=[
            pl.BlockSpec((3, length, PAIR), lambda i, q: (0, q, i)),
            pl.BlockSpec((8, PAIR), lambda i, q: (0, i)),
        ],
        out_shape=[jax.ShapeDtypeStruct((3, rows, width), bf16), jax.ShapeDtypeStruct((8, width), f32)],
        compiler_params=params(),
        cost_estimate=cost(20 * rows * length * width, 16 * rows * width, rows * length * width // HEAD_DIM),
        name="attend_back",
    )(info, qkv, qkv, qkv, context_grad, context, lse)


def input_grad_kernel(grads, qkv_w, grad_one, *outs):
    width = grad_one.shape[1]
    total = grad_one[...]
    for third in range(3):
        total = total + nt(grads[third], qkv_w[:, third * width : (third + 1) * width])
    span = outs[0].shape[1]
    for c, out in enumerate(outs):
        out[0] = total[c * span : (c + 1) * span].astype(bf16)


def input_grad(grads, qkv_w, grad_one, per, chunks):
    _, rows, width = grads.shape
    length = rows // per
    span = length // chunks
    return pl.pallas_call(
        input_grad_kernel,
        grid=(per,),
        in_specs=[
            pl.BlockSpec((3, length, width), lambda i: (0, i, 0)),
            whole(qkv_w.shape),
            pl.BlockSpec((length, width), lambda i: (i, 0)),
        ],
        out_specs=[pl.BlockSpec((1, span, width), lambda i: (i, 0, 0))] * chunks,
        out_shape=[jax.ShapeDtypeStruct((per, span, width), bf16)] * chunks,
        compiler_params=params(),
        cost_estimate=cost(6 * rows * width * width, 12 * rows * width + 6 * width * width),
        name="input_grad",
    )(grads, qkv_w, grad_one)


def weight_grad_kernel(info, left, right, keep, send, left_t, total, *, order, chunk):
    @pl.when(pl.program_id(0) == 0)
    def _():
        left_t[...] = jnp.transpose(left[...])

    rights = right[0] if len(right.shape) == 3 else right[...]
    total[...] = nn(left_t[...], rights)
    me = info[0]
    half = len(order) // 2
    for at in range(0, len(order), 2):
        rows = jnp.concatenate(
            [total[pl.ds(pl.multiple_of((me ^ order[at + k]) * chunk, 8), chunk), :] for k in range(2)], axis=0
        )
        target = keep if at < half else send
        row = (at % half) * chunk
        target[row : row + 2 * chunk, :] = rows.astype(bf16)


def weight_grad(me, left, right, order, tile):
    rows, depth = left.shape
    parts = right.shape[0] if right.ndim == 3 else 1
    width = right.shape[-1]
    chunk = depth // len(order)
    each = width // tile
    if right.ndim == 3:
        spec = pl.BlockSpec((1, rows, tile), lambda j: (j // each, 0, j % each))
    else:
        spec = pl.BlockSpec((rows, tile), lambda j: (0, j))
    return pl.pallas_call(
        functools.partial(weight_grad_kernel, order=order, chunk=chunk),
        grid=(parts * each,),
        in_specs=[smem(), pl.BlockSpec((rows, depth), lambda j: (0, 0)), spec],
        out_specs=[pl.BlockSpec((depth // 2, tile), lambda j: (0, j))] * 2,
        out_shape=[jax.ShapeDtypeStruct((depth // 2, parts * width), bf16)] * 2,
        scratch_shapes=[pltpu.VMEM((depth, rows), bf16), pltpu.VMEM((depth, tile), f32)],
        compiler_params=params(),
        cost_estimate=cost(
            2 * rows * depth * parts * width, 2 * rows * (depth + parts * width) + 2 * depth * parts * width
        ),
        name="weight_grad",
    )(me, left, right)


def halving_order(stages, n_seq):
    bits = [bit * (n_seq if axis == "dp" else 1) for axis, bit in stages]
    count = len(bits)
    return [
        sum(bit for at, bit in enumerate(bits) if (place >> (count - 1 - at)) & 1) for place in range(1 << count)
    ]


def halving_sum(keep, send, stages):
    for at, (axis, bit) in enumerate(stages):
        size = lax.axis_size(axis)
        got = lax.ppermute(send, axis, [(i, i ^ bit) for i in range(size)])
        if at == len(stages) - 1:
            return keep.astype(f32) + got.astype(f32)
        half = keep.shape[0] // 2
        send = (keep[half:].astype(f32) + got[half:].astype(f32)).astype(bf16)
        keep = (keep[:half].astype(f32) + got[:half].astype(f32)).astype(bf16)


def summed_grad(me, left, right, stages, tile):
    n_seq = lax.axis_size("seq")
    n_all = lax.axis_size("dp") * n_seq
    if left.shape[1] % (8 * n_all):
        wide = jnp.concatenate(list(right), axis=1) if right.ndim == 3 else right
        return lax.psum_scatter(tn(left, wide), ("dp", "seq"), scatter_dimension=0, tiled=True)
    keep, send = weight_grad(me, left, right, halving_order(stages, n_seq), tile)
    return halving_sum(keep, send, stages)


def bits_of(size):
    return [1 << k for k in range(size.bit_length() - 1)]


def shards(
    hidden_in,
    lengths,
    labels,
    out_cotangent,
    qkv_weight,
    out_weight,
    up_weight,
    down_weight,
    pool_weight,
    class_weight,
    norm_gains,
    biases,
    up_bias,
    class_bias,
):
    positions, group, width = hidden_in.shape
    n_seq = lax.axis_size("seq")
    n_dp = lax.axis_size("dp")
    n_all = n_seq * n_dp
    seq_at = lax.axis_index("seq")
    me = lax.axis_index("dp") * n_seq + seq_at
    per = group // n_seq
    own_lengths = lax.dynamic_slice_in_dim(lengths, seq_at * per, per)
    info = jnp.concatenate([seq_at[None].astype(jnp.int32), own_lengths, labels])
    me_info = me[None].astype(jnp.int32)
    classes = class_weight.shape[1]
    class_rows = jnp.zeros((128, width), bf16).at[:classes].set(class_weight.T)
    class_shift = jnp.full((1, 128), neg_big, f32).at[0, :classes].set(class_bias)

    x_parts = exchange(split_rows(info, hidden_in.reshape(positions * group, width), positions, group, n_seq))
    cots = exchange(split_rows(info, out_cotangent.reshape(positions * group, width), positions, group, n_seq))

    x_rows, qkv, context, lse, n_one, q_one = attend(info, x_parts, qkv_weight, out_weight, biases)
    outs = feed(
        info, n_one, up_weight, up_bias[None, :], down_weight, norm_gains, biases, pool_weight,
        class_rows, class_shift, per, n_seq,
    )
    middle_low, act, slope, n_two, q_two, record = outs[:6]
    hidden_out = merge_rows(info, exchange(outs[6:]), bf16)

    branch_grad, pre_grad, grad_one, mix_grad, context_grad, sums, up_sums = feed_back(
        info, cots, record, n_two, q_two, slope, down_weight, up_weight, out_weight, n_one, q_one, norm_gains
    )
    seq_bits = [("seq", b) for b in bits_of(n_seq)]
    dp_bits = [("dp", b) for b in bits_of(n_dp)]
    by_dp = seq_bits[:1] + dp_bits[:1] + seq_bits[1:] + dp_bits[1:]
    by_seq = seq_bits + dp_bits
    down_sum = summed_grad(me_info, act, branch_grad, by_dp, 256)
    up_sum = summed_grad(me_info, middle_low, pre_grad, by_seq, 512)
    grads, qkv_sums = attend_back(info, qkv, context_grad, context, lse, n_seq)
    out_sum = summed_grad(me_info, context, mix_grad, by_seq, 384)
    qkv_sum = summed_grad(me_info, x_rows, grads, by_dp, 384)
    grad_in = merge_rows(info, exchange(input_grad(grads, qkv_weight, grad_one, per, n_seq)), f32)

    chunk = width // n_all
    vectors = jnp.concatenate([sums[:6], qkv_sums[:2]], axis=0).reshape(8, n_all, chunk)
    vectors = jnp.concatenate(
        [jnp.transpose(vectors, (1, 0, 2)).reshape(n_all, 8 * chunk), up_sums.reshape(n_all, -1)], axis=1
    )
    vector_sum = lax.psum_scatter(vectors, ("dp", "seq"), scatter_dimension=0, tiled=True)[0]
    vec = vector_sum[: 8 * chunk].reshape(8, chunk)
    up_bias_sum = vector_sum[8 * chunk :]

    records = lax.all_gather(record, ("dp", "seq"), axis=0, tiled=True).reshape(n_all * per, REC, width)
    mine = lax.dynamic_slice_in_dim(records, me * chunk, chunk, axis=2)
    g_logits_all = records[:, 5, :classes]
    pool_sum = lax.dot_general(mine[:, 0], records[:, 1], (((0,), (0,)), ((), ())), precision=highest)
    class_sum = lax.dot_general(mine[:, 2], g_logits_all, (((0,), (0,)), ((), ())), precision=highest)
    pool_bias_sum = jnp.sum(mine[:, 1], axis=0)
    class_bias_sum = jnp.sum(g_logits_all, axis=0)
    ramp_logits = record.reshape(per, REC, width)[:, 4, :classes]

    gains_sum = jnp.stack([vec[3], vec[0]])
    biases_sum = jnp.stack([vec[6], vec[7], vec[4], vec[5], vec[1], vec[2], pool_bias_sum])
    return (
        hidden_out.reshape(positions, group, width),
        ramp_logits,
        grad_in.reshape(positions, group, width),
        qkv_sum,
        out_sum,
        up_sum,
        down_sum,
        pool_sum,
        class_sum,
        gains_sum,
        biases_sum,
        up_bias_sum,
        class_bias_sum,
    )


def solution(mesh):
    every = ("dp", "seq")
    rows = P("seq", "dp", None)
    return jax.shard_map(
        shards,
        mesh=mesh,
        in_specs=(rows, P("dp"), P(every), rows) + (P(),) * 10,
        out_specs=(
            rows,
            P(every, None),
            rows,
            P(every, None),
            P(every, None),
            P(every, None),
            P(every, None),
            P(every, None),
            P(every, None),
            P(None, every),
            P(None, every),
            P(every),
            P(),
        ),
        check_vma=False,
    )
```

time: 1110 us -> 383 us (0.35)
  waiting for transfers between devices: 535 us -> 79.9 us
  matrix products: 210 us -> 1.7 us
  local copies, waits for them, and re-layouts: 204 us -> 11 us
  Pallas kernels: 0 us -> 178 us
  other arithmetic: 61.9 us -> 22.8 us
  blocking collectives: 59 us -> 40.2 us
  starting transfers between devices: 11.4 us -> 29.6 us
    reduce_scatter x5 -> x0, waiting for transfers between devices: 227 us -> none  [the longest x1 105 us: shards(): lax.psum_scatter(grad_out_w, ('dp', 'seq'), scatter_dimension=0, tiled=True)]
    dot_general x74 -> x2, matrix products: 210 us -> 1.7 us  [the longest x1 0.9 us: shards(): lax.dot_general(mine[:, 0], records[:, 1], (((0,), (0,)), ((), ())), prec...]
    pallas_call x0 -> x13, Pallas kernels: none -> 178 us  [the longest x4 37.6 us: weight_grad(): pl.pallas_call(functools.partial(weight_grad_kernel, order=order, chunk=c...]
    all_to_all x2 -> x0, waiting for transfers between devices: 162 us -> none  [the longest x1 109 us: shards(): lax.all_to_all(qkv_grad_pos, 'seq', split_axis=0, concat_axis=2, tiled=True)]
    unnamed x8 -> x1, waiting for transfers between devices: 125 us -> 0.02 us
    reshape x7 -> x3, local copies, waits for them, and re-layouts: 99.6 us -> 0.27 us  [the longest x1 0.11 us: shards(): jnp.concatenate([sums[:6], qkv_sums[:2]], axis=0).reshape(8, n_all, chunk)]
    ppermute x0 -> x32, waiting for transfers between devices: none -> 79.9 us  [the longest x20 59.8 us: halving_sum(): got = lax.ppermute(send, axis, [(i, i ^ bit) for i in range(size)])]
    ppermute x0 -> x32, starting transfers between devices: none -> 29.6 us  [the longest x20 19.3 us: halving_sum(): got = lax.ppermute(send, axis, [(i, i ^ bit) for i in range(size)])]
  transfers between devices with their start and end apart: 9 -> 33, of which waited for: 7 -> 14; matrix products, arithmetic and copies ran while one was open for 23% -> 8% of each run, Pallas kernels for 0% -> 46%
where the time goes in v1:
time: 383 us; the launch traced here: 378 us
  Pallas kernels  178 us (46%)
  waiting for transfers between devices  79.9 us (21%)
  blocking collectives  40.2 us (10%)
  starting transfers between devices  29.6 us (8%)
  other arithmetic  22.8 us (6%)
  between operations  14.6 us (4%)
  local copies, waits for them, and re-layouts  11 us (3%)
    ppermute x20, waiting for transfers between devices, halving_sum(): got = lax.ppermute(send, axis, [(i, i ^ bit) for i in range(size)])  59.8 us
    unnamed x1, blocking collectives  40.2 us
    pallas_call x4, Pallas kernels, weight_grad(): pl.pallas_call(functools.partial(weight_grad_kernel, order=order, chunk=c...  37.6 us
    pallas_call x1, Pallas kernels, feed(): pl.pallas_call(feed_kernel, grid=(per,), in_specs=[smem(), pl.BlockSpec((...  30.8 us
    pallas_call x1, Pallas kernels, attend_back(): pl.pallas_call(functools.partial(attend_back_kernel, chunks=chunks), grid...  30.5 us
    pallas_call x1, Pallas kernels, attend(): pl.pallas_call(attend_kernel, grid=(per,), in_specs=[smem()] + [pl.BlockS...  28.1 us
    pallas_call x1, Pallas kernels, feed_back(): pl.pallas_call(feed_back_kernel, grid=(per,), in_specs=[smem()] + [pl.Blo...  25.8 us
    ppermute x12, waiting for transfers between devices, exchange(): lax.ppermute(parts[c], 'seq', [(i, i ^ c) for i in range(size)])  20.1 us
  transfers between devices with their start and end apart: 33, of which 14 were waited for; matrix products, arithmetic and copies ran while one was open for 8% of the time, Pallas kernels for 46%

profile of v1, /device:TPU:0, one launch (start us, length us, event | category | flops | bytes accessed | tf_op | source)
XLA Modules:
  0.0 377.5 jit_solution(15532664634694370497)
XLA Ops:
  9.2 4.0 %split_rows.2 = (bf16[2,128,768]{2,1,0:T(8,128)(2,1)}, bf16[2,128,768]{2,1,0:T(8,128)(2,1)}, bf16[2,128,768]{2,1,0:T(8,128)(2,1)}, bf16[2,128,768]{2,1,0:T(8,128)(2,1)}) custom-call(s32[5]{0:T(128)} %pad_add_fusion.info, bf16[1024,768]{1,0:T(8,128)(2,1)} %bitcast.30), custom_call_target="tpu_custom_call" | custom-call | flops 201326592 | bytes 3145728 | tf_op jit(solution)/shard_map/split_rows/pallas_call | solution.py:91
  16.3 4.1 %split_rows.3 = (bf16[2,128,768]{2,1,0:T(8,128)(2,1)}, bf16[2,128,768]{2,1,0:T(8,128)(2,1)}, bf16[2,128,768]{2,1,0:T(8,128)(2,1)}, bf16[2,128,768]{2,1,0:T(8,128)(2,1)}) custom-call(s32[5]{0:T(128)} %pad_add_fusion.info, bf16[1024,768]{1,0:T(8,128)(2,1)} %bitcast.31), custom_call_target="tpu_custom_call" | custom-call | flops 201326592 | bytes 3145728 | tf_op jit(solution)/shard_map/split_rows/pallas_call | solution.py:91
  26.4 8.0 %collective-permute-done.2.refs_3_ = bf16[2,128,768]{2,1,0:T(8,128)(2,1)S(1)} collective-permute-done((bf16[2,128,768]{2,1,0:T(8,128)(2,1)}, bf16[2,128,768]{2,1,0:T(8,128)(2,1)S(1)}, u32[]{:S(2)}, u32[]{:S(2)}) %collective-permute-start.2) | collective-permute-done | bytes 393248 | tf_op jit(solution)/shard_map/ppermute | solution.py:143
  35.2 28.1 %attend.1 = (bf16[1024,768]{1,0:T(8,128)(2,1)}, bf16[1024,2304]{1,0:T(8,128)(2,1)}, bf16[1024,768]{1,0:T(8,128)(2,1)}, f32[2,16,512]{2,1,0:T(8,128)}, f32[1024,768]{1,0:T(8,128)}, /*index=5*/f32[1024,1]{1,0:T(8,128)}) custom-call(s32[5]{0:T(128)} %pad_add_fusion.info, bf16[2,128,768]{2,1,0:T(8,128)(2,1)} %get-tuple-element.82.refs_0_, ...), custom_call_target="tpu_custom_call" | custom-call | flops 8053063680 | bytes 20447232 | tf_op jit(solution)/shard_map/attend/pallas_call | solution.py:221
  63.3 30.8 %feed.1 = (bf16[1024,768]{1,0:T(8,128)(2,1)}, bf16[1024,3072]{1,0:T(8,128)(2,1)}, bf16[1024,3072]{1,0:T(8,128)(2,1)}, f32[1024,768]{1,0:T(8,128)}, f32[1024,1]{1...) custom-call(s32[5]{0:T(128)} %pad_add_fusion.info, ...), custom_call_target="tpu_custom_call" | custom-call | flops 9663676416 | bytes 31457280 | tf_op jit(solution)/shard_map/feed/pallas_call | solution.py:317
  95.1 25.8 %feed_back.1 = (bf16[1024,768]{1,0:T(8,128)(2,1)}, bf16[1024,3072]{1,0:T(8,128)(2,1)}, f32[1024,768]{1,0:T(8,128)}, bf16[1024,768]{1,0:T(8,128)(2,1)}, bf16[1024...) custom-call(s32[5]{0:T(128)} %pad_add_fusion.info, bf16[2,128,768]{2,1,0:T(8,128)(2,1)} %get-tuple-element.93.refs_0_, ...), custom_call_target="tpu_custom_call" | custom-call | flops 10871635968 | bytes 37748736 | tf_op jit(solution)/shard_map/feed_back/pallas_call | solution.py:408
  121.0 12.0 %weight_grad.7 = (bf16[1536,768]{1,0:T(8,128)(2,1)}, bf16[1536,768]{1,0:T(8,128)(2,1)}) custom-call(s32[1]{0:T(128)} %bitcast.10.info, bf16[1024,3072]{1,0:T(8,128)(2,1)} %get-tuple-element.120.left, bf16[1024,768]{1,0:T(8,128)(2,1)} %get-tuple-element.121.right), custom_call_target="tpu_custom_call" | custom-call | flops 4831838208 | bytes 12582912 | tf_op jit(solution)/shard_map/weight_grad/pallas_call | solution.py:592
  133.2 5.1 %weight_grad.5 = (bf16[384,768]{1,0:T(8,128)(2,1)}, bf16[384,768]{1,0:T(8,128)(2,1)}) custom-call(s32[1]{0:T(128)} %bitcast.10.info, bf16[1024,768]{1,0:T(8,128)(2,1)} %get-tuple-element.102.context.left, bf16[1024,768]{1,0:T(8,128)(2,1)} %get-tuple-element.113.right), custom_call_target="tpu_custom_call" | custom-call | flops 1207959552 | bytes 4325376 | tf_op jit(solution)/shard_map/weight_grad/pallas_call | solution.py:592
  138.5 30.5 %attend_back.1 = (bf16[3,1024,768]{2,1,0:T(8,128)(2,1)}, f32[8,768]{1,0:T(8,128)}) custom-call(s32[5]{0:T(128)} %pad_add_fusion.info, bf16[1024,2304]{1,0:T(8,128)(2,1)} %get-tuple-element.92.queries_in.keys_in.values_in, bf16[1024,2304]{1,0:T(8,128)(2,1)} %get-tuple-element.92.queries_in.keys_in.values_in, ...), custom_call_target="tpu_custom_call" | custom-call | flops 8053063680 | bytes 12582912 | tf_op jit(solution)/shard_map/attend_back/pallas_call | solution.py:511
  169.0 10.0 %weight_grad.4 = (bf16[384,2304]{1,0:T(8,128)(2,1)}, bf16[384,2304]{1,0:T(8,128)(2,1)}) custom-call(s32[1]{0:T(128)} %bitcast.10.info, bf16[1024,768]{1,0:T(8,128)(2,1)} %get-tuple-element.110.left, bf16[3,1024,768]{2,1,0:T(8,128)(2,1)} %get-tuple-element.104.grads.right), custom_call_target="tpu_custom_call" | custom-call | flops 3623878656 | bytes 9830400 | tf_op jit(solution)/shard_map/weight_grad/pallas_call | solution.py:592
  181.4 8.1 %input_grad.1 = (bf16[2,128,768]{2,1,0:T(8,128)(2,1)}, bf16[2,128,768]{2,1,0:T(8,128)(2,1)}, bf16[2,128,768]{2,1,0:T(8,128)(2,1)}, bf16[2,128,768]{2,1,0:T(8,128)(2,1)}) custom-call(bf16[3,1024,768]{2,1,0:T(8,128)(2,1)} %get-tuple-element.104.grads.right, bf16[768,2304]{1,0:T(8,128)(2,1)} %qkv_w.1, f32[1024,768]{1,0:T(8,128)} %get-tuple-element.105.grad_one), custom_call_target="tpu_custom_call" | custom-call | flops 3623878656 | bytes 12976128 | tf_op jit(solution)/shard_map/input_grad/pallas_call | solution.py:548
  192.9 10.6 %weight_grad.6 = (bf16[384,3072]{1,0:T(8,128)(2,1)}, bf16[384,3072]{1,0:T(8,128)(2,1)}) custom-call(s32[1]{0:T(128)} %bitcast.10.info, bf16[1024,768]{1,0:T(8,128)(2,1)} %get-tuple-element.116.left, bf16[1024,3072]{1,0:T(8,128)(2,1)} %get-tuple-element.117.right), custom_call_target="tpu_custom_call" | custom-call | flops 4831838208 | bytes 12582912 | tf_op jit(solution)/shard_map/weight_grad/pallas_call | solution.py:592
  211.2 40.2 %all-reduce.2 = f32[32,288]{1,0:T(8,128)S(1)} all-reduce(f32[32,288]{1,0:T(8,128)S(1)} %pad_maximum_fusion), channel_id=2, replica_groups=mesh['dp'=8,'seq'=4] {'dp','seq'}, use_global_device_ids=true, to_apply=%region_1.0.clone | all-reduce | flops 9216 | bytes 73728
  258.3 7.8 %collective-permute-done.4.refs_2_ = bf16[2,128,768]{2,1,0:T(8,128)(2,1)S(1)} collective-permute-done((bf16[2,128,768]{2,1,0:T(8,128)(2,1)}, bf16[2,128,768]{2,1,0:T(8,128)(2,1)S(1)}, u32[]{:S(2)}, u32[]{:S(2)}) %collective-permute-start.4) | collective-permute-done | bytes 393248 | tf_op jit(solution)/shard_map/ppermute | solution.py:143
  267.4 4.4 %merge_rows.3 = f32[1024,768]{1,0:T(8,128)} custom-call(s32[5]{0:T(128)} %pad_add_fusion.info, bf16[2,128,768]{2,1,0:T(8,128)(2,1)} %get-tuple-element.106.refs_0_, bf16[2,128,768]{2,1,0:T(8,128)(2,1)} %collective-permute-done.9.refs_1_, bf16[2,128,768]{2,1,0:T(8,128)(2,1)} %copy-done.4, bf16[2,128,768]{2,1,0:T(8,128)(2,1)} %copy-done.5), custom_call_target="tpu_custom_call" | custom-call | flops 201326592 | bytes 4718592 | tf_op jit(solution)/shard_map/merge_rows/pallas_call | solution.py:128
  272.8 4.2 %merge_rows.2 = bf16[1024,768]{1,0:T(8,128)(2,1)} custom-call(s32[5]{0:T(128)} %pad_add_fusion.info, bf16[2,128,768]{2,1,0:T(8,128)(2,1)} %get-tuple-element.87.refs_0_, bf16[2,128,768]{2,1,0:T(8,128)(2,1)} %collective-permute-done.3.refs_1_, bf16[2,128,768]{2,1,0:T(8,128)(2,1)} %copy-done.6, bf16[2,128,768]{2,1,0:T(8,128)(2,1)} %copy-done.7), custom_call_target="tpu_custom_call" | custom-call | flops 201326592 | bytes 4718592 | tf_op jit(solution)/shard_map/merge_rows/pallas_call | solution.py:128
  283.7 3.5 add_convert_fusion.3
  288.7 13.5 %collective-permute-done.13 = bf16[192,2304]{1,0:T(8,128)(2,1)S(1)} collective-permute-done((bf16[192,2304]{1,0:T(8,128)(2,1)S(1)}, bf16[192,2304]{1,0:T(8,128)(2,1)S(1)}, u32[]{:S(2)}, u32[]{:S(2)}) %collective-permute-start.13) | collective-permute-done | bytes 884768 | tf_op jit(solution)/shard_map/ppermute | solution.py:618
  312.3 12.6 %collective-permute-done.14 = bf16[96,2304]{1,0:T(8,128)(2,1)S(1)} collective-permute-done((bf16[96,2304]{1,0:T(8,128)(2,1)}, bf16[96,2304]{1,0:T(8,128)(2,1)S(1)}, u32[]{:S(2)}, u32[]{:S(2)}) %collective-permute-start.14) | collective-permute-done | bytes 442400 | tf_op jit(solution)/shard_map/ppermute | solution.py:618
  334.1 9.6 %collective-permute-done.29 = bf16[384,768]{1,0:T(8,128)(2,1)S(1)} collective-permute-done((bf16[384,768]{1,0:T(8,128)(2,1)S(1)}, bf16[384,768]{1,0:T(8,128)(2,1)S(1)}, u32[]{:S(2)}, u32[]{:S(2)}) %collective-permute-start.29) | collective-permute-done | bytes 589856 | tf_op jit(solution)/shard_map/ppermute | solution.py:618
  343.9 2.9 collective-permute-done.24
  347.8 7.7 %collective-permute-done.30 = bf16[192,768]{1,0:T(8,128)(2,1)S(1)} collective-permute-done((bf16[192,768]{1,0:T(8,128)(2,1)S(1)}, bf16[192,768]{1,0:T(8,128)(2,1)S(1)}, u32[]{:S(2)}, u32[]{:S(2)}) %collective-permute-start.30) | collective-permute-done | bytes 294944 | tf_op jit(solution)/shard_map/ppermute | solution.py:618
  355.6 4.0 %collective-permute-done.25 = bf16[48,3072]{1,0:T(8,128)(2,1)S(1)} collective-permute-done((bf16[48,3072]{1,0:T(8,128)(2,1)S(1)}, bf16[48,3072]{1,0:T(8,128)(2,1)S(1)}, u32[]{:S(2)}, u32[]{:S(2)}) %collective-permute-start.25) | collective-permute-done | bytes 294944 | tf_op jit(solution)/shard_map/ppermute | solution.py:618
  361.2 6.5 %collective-permute-done.31 = bf16[96,768]{1,0:T(8,128)(2,1)S(1)} collective-permute-done((bf16[96,768]{1,0:T(8,128)(2,1)S(1)}, bf16[96,768]{1,0:T(8,128)(2,1)S(1)}, u32[]{:S(2)}, u32[]{:S(2)}) %collective-permute-start.31) | collective-permute-done | bytes 147488 | tf_op jit(solution)/shard_map/ppermute | solution.py:618
  (142 shorter events, 69.1 us)
Async XLA Ops:
  7.2 297.8 %all-gather.2.cloned.1.call-start = ((), (), s32[]{:S(2)}) async-start(), calls=%async_computation | async-start | bytes 1622016 | tf_op jit(solution)/shard_map/all_gather | solution.py:704
  13.7 12.7 %collective-permute-start.1 = (bf16[2,128,768]{2,1,0:T(8,128)(2,1)}, bf16[2,128,768]{2,1,0:T(8,128)(2,1)S(1)}, u32[]{:S(2)}, u32[]{:S(2)}) collective-permute-start(bf16[2,128,768]{2,1,0:T(8,128)(2,1)} %get-tuple-element.84), channel_id=1, source_target_pairs={{0,2},{1,3},{2,0},{3,1},{4,6},{5,7},{6,4},{7,5},{8,10},{9,11},{10,... | collective-permute-start | bytes 1179656 | tf_op jit(solution)/shard_map/ppermute | solution.py:143
  16.2 18.2 %collective-permute-start.2 = (bf16[2,128,768]{2,1,0:T(8,128)(2,1)}, bf16[2,128,768]{2,1,0:T(8,128)(2,1)S(1)}, u32[]{:S(2)}, u32[]{:S(2)}) collective-permute-start(bf16[2,128,768]{2,1,0:T(8,128)(2,1)} %get-tuple-element.85), channel_id=1, source_target_pairs={{0,3},{1,2},{2,1},{3,0},{4,7},{5,6},{6,5},{7,4},{8,11},{9,10},{10,... | collective-permute-start | bytes 1179656 | tf_op jit(solution)/shard_map/ppermute | solution.py:143
  20.5 73.6 %collective-permute-start.6 = (bf16[2,128,768]{2,1,0:T(8,128)(2,1)}, bf16[2,128,768]{2,1,0:T(8,128)(2,1)S(1)}, u32[]{:S(2)}, u32[]{:S(2)}) collective-permute-start(bf16[2,128,768]{2,1,0:T(8,128)(2,1)} %get-tuple-element.94), channel_id=1, source_target_pairs={{0,1},{1,0},{2,3},{3,2},{4,5},{5,4},{6,7},{7,6},{8,9},{9,8},{10,11... | collective-permute-start | bytes 1179656 | tf_op jit(solution)/shard_map/ppermute | solution.py:143
  20.6 73.5 %collective-permute-start.7 = (bf16[2,128,768]{2,1,0:T(8,128)(2,1)}, bf16[2,128,768]{2,1,0:T(8,128)(2,1)S(1)}, u32[]{:S(2)}, u32[]{:S(2)}) collective-permute-start(bf16[2,128,768]{2,1,0:T(8,128)(2,1)} %get-tuple-element.95), channel_id=1, source_target_pairs={{0,2},{1,3},{2,0},{3,1},{4,6},{5,7},{6,4},{7,5},{8,10},{9,11},{10,... | collective-permute-start | bytes 1179656 | tf_op jit(solution)/shard_map/ppermute | solution.py:143
  25.0 69.1 %collective-permute-start.8 = (bf16[2,128,768]{2,1,0:T(8,128)(2,1)}, bf16[2,128,768]{2,1,0:T(8,128)(2,1)S(1)}, u32[]{:S(2)}, u32[]{:S(2)}) collective-permute-start(bf16[2,128,768]{2,1,0:T(8,128)(2,1)} %get-tuple-element.96), channel_id=1, source_target_pairs={{0,3},{1,2},{2,1},{3,0},{4,7},{5,6},{6,5},{7,4},{8,11},{9,10},{10,... | collective-permute-start | bytes 1179656 | tf_op jit(solution)/shard_map/ppermute | solution.py:143
  132.9 148.7 %collective-permute-start.27 = (bf16[1536,768]{1,0:T(8,128)(2,1)}, bf16[1536,768]{1,0:T(8,128)(2,1)S(1)}, u32[]{:S(2)}, u32[]{:S(2)}) collective-permute-start(bf16[1536,768]{1,0:T(8,128)(2,1)} %get-tuple-element.123), channel_id=1, source_target_pairs={{0,1},{1,0},{2,3},{3,2},{4,5},{5,4},{6,7},{7,6},{8,9},{9,8},{10,11... | collective-permute-start | bytes 7077896 | tf_op jit(solution)/shard_map/ppermute | solution.py:618
  138.3 41.0 %collective-permute-start.17 = (bf16[384,768]{1,0:T(8,128)(2,1)}, bf16[384,768]{1,0:T(8,128)(2,1)S(1)}, u32[]{:S(2)}, u32[]{:S(2)}) collective-permute-start(bf16[384,768]{1,0:T(8,128)(2,1)} %get-tuple-element.115), channel_id=1, source_target_pairs={{0,1},{1,0},{2,3},{3,2},{4,5},{5,4},{6,7},{7,6},{8,9},{9,8},{10,11... | collective-permute-start | bytes 1769480 | tf_op jit(solution)/shard_map/ppermute | solution.py:618
  179.0 98.6 %collective-permute-start.12 = (bf16[384,2304]{1,0:T(8,128)(2,1)}, bf16[384,2304]{1,0:T(8,128)(2,1)}, u32[]{:S(2)}, u32[]{:S(2)}) collective-permute-start(bf16[384,2304]{1,0:T(8,128)(2,1)} %get-tuple-element.112), channel_id=1, source_target_pairs={{0,1},{1,0},{2,3},{3,2},{4,5},{5,4},{6,7},{7,6},{8,9},{9,8},{10,11... | collective-permute-start | bytes 5308424 | tf_op jit(solution)/shard_map/ppermute | solution.py:618
  189.5 14.7 %collective-permute-start.10 = (bf16[2,128,768]{2,1,0:T(8,128)(2,1)}, bf16[2,128,768]{2,1,0:T(8,128)(2,1)S(1)}, u32[]{:S(2)}, u32[]{:S(2)}) collective-permute-start(bf16[2,128,768]{2,1,0:T(8,128)(2,1)} %get-tuple-element.108), channel_id=1, source_target_pairs={{0,2},{1,3},{2,0},{3,1},{4,6},{5,7},{6,4},{7,5},{8,10},{9,11},{10,... | collective-permute-start | bytes 1179656 | tf_op jit(solution)/shard_map/ppermute | solution.py:143
  189.6 18.1 %collective-permute-start.11 = (bf16[2,128,768]{2,1,0:T(8,128)(2,1)}, bf16[2,128,768]{2,1,0:T(8,128)(2,1)S(1)}, u32[]{:S(2)}, u32[]{:S(2)}) collective-permute-start(bf16[2,128,768]{2,1,0:T(8,128)(2,1)} %get-tuple-element.109), channel_id=1, source_target_pairs={{0,3},{1,2},{2,1},{3,0},{4,7},{5,6},{6,5},{7,4},{8,11},{9,10},{10,... | collective-permute-start | bytes 1179656 | tf_op jit(solution)/shard_map/ppermute | solution.py:143
  191.3 19.0 %collective-permute-start.19 = (bf16[96,768]{1,0:T(8,128)(2,1)}, bf16[96,768]{1,0:T(8,128)(2,1)S(1)}, u32[]{:S(2)}, u32[]{:S(2)}) collective-permute-start(bf16[96,768]{1,0:T(8,128)(2,1)} %get-tuple-element.153), channel_id=1, source_target_pairs={{0,4},{4,0},{8,12},{12,8},{16,20},{20,16},{24,28},{28,24},{1,5},{5... | collective-permute-start | bytes 442376 | tf_op jit(solution)/shard_map/ppermute | solution.py:618
  204.2 79.2 %collective-permute-start.22 = (bf16[384,3072]{1,0:T(8,128)(2,1)}, bf16[384,3072]{1,0:T(8,128)(2,1)}, u32[]{:S(2)}, u32[]{:S(2)}) collective-permute-start(bf16[384,3072]{1,0:T(8,128)(2,1)} %get-tuple-element.119), channel_id=1, source_target_pairs={{0,1},{1,0},{2,3},{3,2},{4,5},{5,4},{6,7},{7,6},{8,9},{9,8},{10,11... | collective-permute-start | bytes 7077896 | tf_op jit(solution)/shard_map/ppermute | solution.py:618
  207.7 43.8 %collective-permute-start.9 = (bf16[2,128,768]{2,1,0:T(8,128)(2,1)}, bf16[2,128,768]{2,1,0:T(8,128)(2,1)}, u32[]{:S(2)}, u32[]{:S(2)}) collective-permute-start(bf16[2,128,768]{2,1,0:T(8,128)(2,1)} %get-tuple-element.107), channel_id=1, source_target_pairs={{0,1},{1,0},{2,3},{3,2},{4,5},{5,4},{6,7},{7,6},{8,9},{9,8},{10,11... | collective-permute-start | bytes 1179656 | tf_op jit(solution)/shard_map/ppermute | solution.py:143
  210.3 43.3 %collective-permute-start.3 = (bf16[2,128,768]{2,1,0:T(8,128)(2,1)}, bf16[2,128,768]{2,1,0:T(8,128)(2,1)}, u32[]{:S(2)}, u32[]{:S(2)}) collective-permute-start(bf16[2,128,768]{2,1,0:T(8,128)(2,1)} %get-tuple-element.88), channel_id=1, source_target_pairs={{0,1},{1,0},{2,3},{3,2},{4,5},{5,4},{6,7},{7,6},{8,9},{9,8},{10,11... | collective-permute-start | bytes 1179656 | tf_op jit(solution)/shard_map/ppermute | solution.py:143
  255.9 16.1 %collective-permute-start.5 = (bf16[2,128,768]{2,1,0:T(8,128)(2,1)}, bf16[2,128,768]{2,1,0:T(8,128)(2,1)S(1)}, u32[]{:S(2)}, u32[]{:S(2)}) collective-permute-start(bf16[2,128,768]{2,1,0:T(8,128)(2,1)} %get-tuple-element.90), channel_id=1, source_target_pairs={{0,3},{1,2},{2,1},{3,0},{4,7},{5,6},{6,5},{7,4},{8,11},{9,10},{10,... | collective-permute-start | bytes 1179656 | tf_op jit(solution)/shard_map/ppermute | solution.py:143
  279.7 22.5 %collective-permute-start.13 = (bf16[192,2304]{1,0:T(8,128)(2,1)S(1)}, bf16[192,2304]{1,0:T(8,128)(2,1)S(1)}, u32[]{:S(2)}, u32[]{:S(2)}) collective-permute-start(bf16[192,2304]{1,0:T(8,128)(2,1)S(1)} %get-tuple-element.132), channel_id=1, source_target_pairs={{0,4},{4,0},{8,12},{12,8},{16,20},{20,16},{24,28},{28,24},{1,5},{5... | collective-permute-start | bytes 2654216 | tf_op jit(solution)/shard_map/ppermute | solution.py:618
  283.2 44.0 %collective-permute-start.28 = (bf16[768,768]{1,0:T(8,128)(2,1)}, bf16[768,768]{1,0:T(8,128)(2,1)}, u32[]{:S(2)}, u32[]{:S(2)}) collective-permute-start(bf16[768,768]{1,0:T(8,128)(2,1)} %get-tuple-element.128), channel_id=1, source_target_pairs={{0,4},{4,0},{8,12},{12,8},{16,20},{20,16},{24,28},{28,24},{1,5},{5... | collective-permute-start | bytes 3538952 | tf_op jit(solution)/shard_map/ppermute | solution.py:618
  287.2 43.3 %collective-permute-start.23 = (bf16[192,3072]{1,0:T(8,128)(2,1)}, bf16[192,3072]{1,0:T(8,128)(2,1)}, u32[]{:S(2)}, u32[]{:S(2)}) collective-permute-start(bf16[192,3072]{1,0:T(8,128)(2,1)} %get-tuple-element.130), channel_id=1, source_target_pairs={{0,2},{1,3},{2,0},{3,1},{4,6},{5,7},{6,4},{7,5},{8,10},{9,11},{10,... | collective-permute-start | bytes 3538952 | tf_op jit(solution)/shard_map/ppermute | solution.py:618
  303.2 21.6 %collective-permute-start.14 = (bf16[96,2304]{1,0:T(8,128)(2,1)}, bf16[96,2304]{1,0:T(8,128)(2,1)S(1)}, u32[]{:S(2)}, u32[]{:S(2)}) collective-permute-start(bf16[96,2304]{1,0:T(8,128)(2,1)} %get-tuple-element.138), channel_id=1, source_target_pairs={{0,2},{1,3},{2,0},{3,1},{4,6},{5,7},{6,4},{7,5},{8,10},{9,11},{10,... | collective-permute-start | bytes 1327112 | tf_op jit(solution)/shard_map/ppermute | solution.py:618
  328.7 15.0 %collective-permute-start.29 = (bf16[384,768]{1,0:T(8,128)(2,1)S(1)}, bf16[384,768]{1,0:T(8,128)(2,1)S(1)}, u32[]{:S(2)}, u32[]{:S(2)}) collective-permute-start(bf16[384,768]{1,0:T(8,128)(2,1)S(1)} %get-tuple-element.134), channel_id=1, source_target_pairs={{0,2},{1,3},{2,0},{3,1},{4,6},{5,7},{6,4},{7,5},{8,10},{9,11},{10,... | collective-permute-start | bytes 1769480 | tf_op jit(solution)/shard_map/ppermute | solution.py:618
  332.1 14.7 %collective-permute-start.24 = (bf16[96,3072]{1,0:T(8,128)(2,1)S(1)}, bf16[96,3072]{1,0:T(8,128)(2,1)S(1)}, u32[]{:S(2)}, u32[]{:S(2)}) collective-permute-start(bf16[96,3072]{1,0:T(8,128)(2,1)S(1)} %get-tuple-element.136), channel_id=1, source_target_pairs={{0,4},{4,0},{8,12},{12,8},{16,20},{20,16},{24,28},{28,24},{1,5},{5... | collective-permute-start | bytes 1769480 | tf_op jit(solution)/shard_map/ppermute | solution.py:618
  332.7 14.3 %collective-permute-start.16 = (bf16[24,2304]{1,0:T(8,128)(2,1)S(1)}, bf16[24,2304]{1,0:T(8,128)(2,1)S(1)}, u32[]{:S(2)}, u32[]{:S(2)}) collective-permute-start(bf16[24,2304]{1,0:T(8,128)(2,1)S(1)} %add_convert_fusion.26), channel_id=1, source_target_pairs={{0,16},{4,20},{8,24},{12,28},{16,0},{20,4},{24,8},{28,12},{1,17},{... | collective-permute-start | bytes 331784 | tf_op jit(solution)/shard_map/ppermute | solution.py:618
  346.9 12.6 %collective-permute-start.25 = (bf16[48,3072]{1,0:T(8,128)(2,1)S(1)}, bf16[48,3072]{1,0:T(8,128)(2,1)S(1)}, u32[]{:S(2)}, u32[]{:S(2)}) collective-permute-start(bf16[48,3072]{1,0:T(8,128)(2,1)S(1)} %get-tuple-element.147), channel_id=1, source_target_pairs={{0,8},{4,12},{8,0},{12,4},{16,24},{20,28},{24,16},{28,20},{1,9},{5... | collective-permute-start | bytes 884744 | tf_op jit(solution)/shard_map/ppermute | solution.py:618
  (29 other events, 279.7 us)
Sparse Core Ops, SparseCore 0:
  94.2 56.5 all-gather.1
